TPU v7x, 128 devices: a whole 4x4x4 slice. The times are simulated.
128 devices in a mesh: tiles: 16 (over x, z), cols: 8 (over y, core).
Axes of the slice: x: 4, y: 4, z: 4, core: 2. Of those that a mesh axis runs over, the one named last changes fastest.
Arguments:
- object_field: float32 [2, 2, 4096, 2048], P(None, None, 'tiles', 'cols')
- probe: float32 [2, 4, 128, 128], replicated, may hold values from -3 to 3
- row_offsets: int32 [16, 8, 8], P('tiles', 'cols'), may hold values from 0 to 255, as said below
- col_offsets: int32 [16, 8, 8], P('tiles', 'cols'), may hold values from 0 to 255, as said below
- counts: int32 [16, 8], P('tiles', 'cols'), may hold values from 1 to 8, as said below
- measured: float32 [16, 8, 8, 128, 128], P('tiles', 'cols'), may hold values from 0.25 to 2.5
Outputs:
- new_object: float32 [2, 2, 4096, 2048], P(None, None, 'tiles', 'cols')
- new_probe: float32 [2, 4, 128, 128], replicated
Inputs may be any that keep to these rules, and one draw needn't show every extreme that they name: `row_offsets`: A patch never leaves the object region: on the last row of tiles the offset is at most 128; elsewhere it may reach into the tile below. `col_offsets`: A patch never leaves the object region: on the last column of tiles the offset is at most 128; elsewhere it may reach into the tile to the right. `counts`: slots from a device's count on are unused; some device has 8 live positions.
All inputs are finite; a program needn't handle non-finite values.
Results may differ from a plain program's by a relative error of at most 0.0001.
Values sent between devices are 32-bit elements; how exact they have to be, the bound alone decides.
A program may use at most 128 MiB of HBM per device.

v0:
```python
import functools
import math

import jax
import jax.numpy as jnp
import ml_dtypes
import numpy as np
from jax import lax
from jax.experimental import pallas as pl
from jax.experimental.pallas import tpu as pltpu
from jax.sharding import PartitionSpec as P

ITERS = 2
STEP_OBJECT = 0.25
f32, bf16 = jnp.float32, jnp.bfloat16
MESH = pl.DeviceIdType.MESH
VMEM_LIMIT = 56 * 2**20

A_PLUS, A_MINUS, F_PLUS, F_MINUS = 0, 2, 4, 6


def split_table(table):
    high = table.astype(np.float32).astype(ml_dtypes.bfloat16)
    low = (table - high.astype(np.float64)).astype(np.float32).astype(ml_dtypes.bfloat16)
    return [high, low]


def transform_tables(size):
    line = np.arange(size)
    dft = np.exp(-2j * np.pi * (np.outer(line, line) % size) / size) / math.sqrt(size)
    freq = np.where(line < size // 2, line, line - size)
    chirp = np.exp(-2j * np.pi * ((freq * freq) % (4 * size)) / (4 * size))
    propagator = np.conj(dft) @ (chirp[:, None] * dft)
    parts = []
    for matrix in (propagator, dft):
        real, imag = matrix.real, matrix.imag
        plus = np.block([[real, imag], [-imag, real]])
        parts += split_table(plus) + split_table(plus.T)
    return np.stack(parts)


def split(value):
    high = value.astype(bf16)
    return high, (value - high.astype(f32)).astype(bf16)


def product(first, second):
    dot = functools.partial(jnp.dot, preferred_element_type=f32)
    return dot(first[0], second[0]) + (dot(first[1], second[0]) + dot(first[0], second[1]))


def two_sided(groups, table, left, right):
    n = groups[0][0][0].shape[0]
    modes = range(len(groups[0]))
    middles = []
    for fields in groups:
        stacked = [jnp.concatenate(field, axis=0) for field in fields]
        middles.append(
            product((table[left], table[left + 1]), split(jnp.concatenate(stacked, axis=1)))
        )
    results = []
    for middle in middles:
        columns = [middle[:, n * m : n * m + n] for m in modes]
        beside = [jnp.concatenate([c[:n], c[n:]], axis=1) for c in columns]
        result = product(split(jnp.concatenate(beside, axis=0)), (table[right], table[right + 1]))
        rows = [result[n * m : n * m + n] for m in modes]
        results.append([(row[:, :n], row[:, n:]) for row in rows])
    return results


def times(a, b):
    return (a[0] * b[0] - a[1] * b[1], a[0] * b[1] + a[1] * b[0])


def conj_times(a, b):
    return (a[0] * b[0] + a[1] * b[1], a[0] * b[1] - a[1] * b[0])


def total(terms):
    real, imag = terms[0]
    for term in terms[1:]:
        real, imag = real + term[0], imag + term[1]
    return real, imag


GROUP = 4
LINE = 4


class Positions:
    def __init__(self, refs, n, slots):
        self.rows, self.cols, self.counts, self.measured = refs[:4]
        self.extended, self.beam, self.table, self.grad, self.grad_beam = refs[4:9]
        self.windows, self.spread, self.patches = refs[9:]
        self.n, self.slots = n, slots
        self.modes = range(self.spread.shape[1])
        self.groups = slots // GROUP

    def beams(self):
        n, part = self.n, len(self.modes) * self.n
        return [(self.beam[pl.ds(m * n, n)], self.beam[pl.ds(part + m * n, n)]) for m in self.modes]

    def spots(self, step):
        found = []
        for k in range(GROUP):
            slot = step * GROUP + k
            live = slot < self.counts[0]
            row = jnp.where(live, self.rows[slot], 0)
            col = jnp.where(live, self.cols[slot], 0)
            block = lax.shift_right_logical(col, 7)
            weight = jnp.where(live, 1.0, 0.0).astype(f32)
            found.append((slot, weight, row, block, col - block * self.n))
        return found

    def lane(self):
        return lax.broadcasted_iota(jnp.int32, (self.n, self.n), 1)

    def window(self, plane, spot):
        n = self.n
        _, _, row, block, shift = spot
        back = jnp.bitwise_and(n - shift, n - 1)
        near = pltpu.roll(self.extended[plane % 2][plane // 2, block, pl.ds(row, n), :], back, 1)
        far = pltpu.roll(self.extended[plane % 2][plane // 2, block + 1, pl.ds(row, n), :], back, 1)
        return jnp.where(self.lane() < n - shift, near, far)

    def propagate(self, step):
        spots, beams = self.spots(step), self.beams()
        first = [(self.window(0, s), self.window(2, s)) for s in spots]
        for spot, field in zip(spots, first):
            self.windows[spot[0], 0], self.windows[spot[0], 1] = field
        fields = [[times(b, field) for b in beams] for field in first]
        results = two_sided(fields, self.table, A_MINUS, A_PLUS)
        for spot, result in zip(spots, results):
            for m in self.modes:
                self.spread[spot[0], m, 0], self.spread[spot[0], m, 1] = result[m]

    def diffract(self, step):
        spots = self.spots(step)
        spread = [
            [(self.spread[s[0], m, 0], self.spread[s[0], m, 1]) for m in self.modes] for s in spots
        ]
        second = [(self.window(1, s), self.window(3, s)) for s in spots]
        leaving = [[times(o, x) for x in fields] for o, fields in zip(second, spread)]
        far = two_sided(leaving, self.table, F_MINUS, F_PLUS)
        residual = []
        for spot, fields in zip(spots, far):
            intensity = sum(y[0] * y[0] + y[1] * y[1] for y in fields)
            residual.append((intensity - self.measured[spot[0]]) * spot[1])
        weighed = [[(r * y[0], r * y[1]) for y in fields] for r, fields in zip(residual, far)]
        back = two_sided(weighed, self.table, F_PLUS, F_MINUS)
        patches = [
            total([conj_times(x, g) for x, g in zip(fields, backs)])
            for fields, backs in zip(spread, back)
        ]
        for spot, patch in zip(spots, patches):
            self.patches[spot[0], 1], self.patches[spot[0], 3] = patch
        entering = [[conj_times(o, g) for g in backs] for o, backs in zip(second, back)]
        back = two_sided(entering, self.table, A_PLUS, A_MINUS)
        beams = self.beams()
        n, part = self.n, len(self.modes) * self.n
        first = [(self.windows[s[0], 0], self.windows[s[0], 1]) for s in spots]
        for m in self.modes:
            terms = total([conj_times(o, backs[m]) for o, backs in zip(first, back)])
            for term, start in zip(terms, (m * n, part + m * n)):
                self.grad_beam[pl.ds(start, n)] += term
        for spot, backs in zip(spots, back):
            patch = total([conj_times(b, g) for b, g in zip(beams, backs)])
            self.patches[spot[0], 0], self.patches[spot[0], 2] = patch

    def place_patches(self, step, planes):
        spots = self.spots(step)
        patches = [[self.patches[s[0], p] for p in planes] for s in spots]
        self.put(spots, patches, planes, step == 0)

    def put(self, spots, patches, planes, fresh):
        n = self.n
        count, tall = self.grad.shape[1:3]
        offset = lax.broadcasted_iota(jnp.int32, (tall, n), 0) - lax.broadcasted_iota(
            jnp.int32, (tall, n), 1
        )
        ones, pieces = [], [[] for _ in range(count)]
        for (_, _, row, block, shift), patch in zip(spots, patches):
            ones += [jnp.where(offset == row, 1.0, 0.0).astype(bf16)] * 2
            kept = self.lane() >= shift
            beside = [[] for _ in range(count)]
            for value in patch:
                moved = pltpu.roll(value, shift, 1)
                near, over = jnp.where(kept, moved, 0.0), jnp.where(kept, 0.0, moved)
                for b in range(count):
                    if b == 0:
                        placed = jnp.where(block == 0, near, 0.0)
                    elif b == count - 1:
                        placed = jnp.where(block == b - 1, over, 0.0)
                    else:
                        placed = jnp.where(block == b, near, jnp.where(block == b - 1, over, 0.0))
                    beside[b].append(placed)
            for b in range(count):
                pieces[b] += split(jnp.concatenate(beside[b], axis=1))
        ones = jnp.concatenate(ones, axis=1)
        for b in range(count):
            sums = jnp.dot(ones, jnp.concatenate(pieces[b], axis=0), preferred_element_type=f32)
            for k, p in enumerate(planes):
                if fresh:
                    self.grad[p, b] = sums[:, k * n : k * n + n]
                else:
                    self.grad[p, b] += sums[:, k * n : k * n + n]


class Place:
    def __init__(self, tiles, cols):
        self.tiles, self.cols = tiles, cols
        self.t, self.c = lax.axis_index("tiles"), lax.axis_index("cols")

    def at(self, down, right):
        return (
            lax.rem(self.t + (down + self.tiles), self.tiles),
            lax.rem(self.c + (right + self.cols), self.cols),
        )


def greet(devices):
    barrier = pltpu.get_barrier_semaphore()
    for device in devices:
        pl.semaphore_signal(barrier, inc=1, device_id=device, device_id_type=MESH)
    pl.semaphore_wait(barrier, len(devices))


class Copies:
    def __init__(self, send, recv):
        self.send, self.recv, self.used, self.started = send, recv, 0, []

    def start(self, source, target, device):
        k = self.used
        self.used += 1
        copy = pltpu.make_async_remote_copy(
            src_ref=source,
            dst_ref=target,
            send_sem=self.send.at[k],
            recv_sem=self.recv.at[k],
            device_id=device,
            device_id_type=MESH,
        )
        copy.start()
        self.started.append(copy)
        return copy

    def sent(self, copy):
        copy.wait_send()
        self.started = [other for other in self.started if other is not copy]

    def finish(self):
        for copy in self.started:
            copy.wait_send()
        self.started = []


class ProbeSum:
    def __init__(self, place, copies, grad, pair, pieces, column, halves):
        self.place, self.copies = place, copies
        self.grad, self.pair, self.pieces, self.column, self.halves = grad, pair, pieces, column, halves
        self.half = grad.shape[0] // 2
        self.piece = self.half // (pieces.shape[0] + 1)
        self.core = lax.rem(place.c, 2)
        self.partner = (place.t, place.c + 1 - 2 * self.core)
        self.mine = pl.ds(self.core * self.half, self.half)
        self.others = pl.ds((1 - self.core) * self.half, self.half)

    @staticmethod
    def plane(place):
        found = []
        chips = place.cols // 2
        for k in range(1, place.tiles // LINE * chips):
            t, c = place.at(k // chips * LINE, 2 * (k % chips))
            found.append((t // LINE * chips + c // 2, (t, c)))
        return found

    @staticmethod
    def line(place):
        start = place.t // LINE * LINE
        return [(start + lax.rem(place.t + k, LINE), place.c) for k in range(1, LINE)]

    def part(self, number):
        return pl.ds(self.core * self.half + number * self.piece, self.piece)

    def number(self):
        return self.place.t // LINE * (self.place.cols // 2) + self.place.c // 2

    def scatter_pair(self):
        self.step = self.copies.start(self.grad.at[self.others], self.pair, self.partner)

    def scatter_plane(self):
        self.step.wait_recv()
        self.grad[self.mine] += self.pair[...]
        self.steps = [
            self.copies.start(self.grad.at[self.part(number)], self.pieces.at[k], device)
            for k, (number, device) in enumerate(self.plane(self.place))
        ]

    def sum_line(self):
        value = self.grad[self.part(self.number())]
        for k, step in enumerate(self.steps):
            step.wait_recv()
            value += self.pieces[k]
        spot = lax.rem(self.place.t, LINE)
        self.column[spot] = value
        self.steps = [
            self.copies.start(self.column.at[spot], self.column.at[spot], device)
            for device in self.line(self.place)
        ]

    def gather_plane(self):
        for step in self.steps:
            step.wait_recv()
        value = self.column[0]
        for k in range(1, LINE):
            value += self.column[k]
        own = self.part(self.number())
        self.halves[own] = value
        self.steps = [
            self.copies.start(self.halves.at[own], self.halves.at[own], device)
            for _, device in self.plane(self.place)
        ]

    def gather_pair(self):
        for step in self.steps:
            step.wait_recv()
        self.step = self.copies.start(
            self.halves.at[self.mine], self.halves.at[self.mine], self.partner
        )

    def result(self):
        self.step.wait_recv()
        return self.halves[...]

    @staticmethod
    def copies_needed(tiles, cols):
        return tiles * cols // (2 * LINE) * 2 + LINE - 1

    @staticmethod
    def scratch(rows, lanes, tiles, cols):
        half = rows // 2
        parts = tiles * cols // (2 * LINE)
        piece = half // parts
        return [
            pltpu.VMEM((half, lanes), f32),
            pltpu.VMEM((parts - 1, piece, lanes), f32),
            pltpu.VMEM((LINE, piece, lanes), f32),
            pltpu.VMEM((rows, lanes), f32),
        ]


def met(place):
    sides = [place.at(*way) for way in ((-1, 0), (1, 0), (0, -1), (0, 1))]
    return [device for _, device in ProbeSum.plane(place)] + ProbeSum.line(place) + sides


class Overlap:
    def __init__(self, place, copies, planes, grad, extended, buffers, final):
        self.place, self.copies, self.planes, self.final = place, copies, planes, final
        self.grad, self.extended = grad, extended
        self.from_left, self.from_up, self.from_right, self.from_down, self.from_corner = buffers
        count, tall, size = grad.shape[1:]
        self.last, height = count - 1, tall - size
        self.top, self.middle = pl.ds(0, size), pl.ds(size, height - size)
        self.below, self.own = pl.ds(height, size), pl.ds(0, height)
        self.block = [pl.ds(j * size, size) for j in range(self.last)]
        self.ups, self.downs = {}, {}

    def rows(self, j):
        up, down = self.place.at(-1, 0), self.place.at(1, 0)
        for p in self.planes:
            self.ups[p, j] = self.copies.start(
                self.grad.at[p, j, self.below], self.from_up.at[p, j], down
            )
            if not self.final:
                self.downs[p, j] = self.copies.start(
                    self.grad.at[p, j, self.top], self.from_down.at[p, j], up
                )

    def start(self):
        right = self.place.at(0, 1)
        self.edges = {
            (p, k): self.copies.start(
                self.grad.at[p, self.last, lines], self.from_left.at[p, lines], right
            )
            for p in self.planes
            for k, lines in enumerate((self.top, self.below))
        }
        for j in range(1, self.last):
            self.rows(j)

    def start_inner(self):
        right = self.place.at(0, 1)
        self.sides = [
            self.copies.start(
                self.grad.at[p, self.last, self.middle], self.from_left.at[p, self.middle], right
            )
            for p in self.planes
        ]

    def first(self):
        for p in self.planes:
            for k, lines in enumerate((self.top, self.below)):
                self.edges[p, k].wait_recv()
                self.grad[p, 0, lines] += self.from_left[p, lines]
        self.rows(0)

    def inner(self):
        left = self.place.at(0, -1)
        self.middles = []
        for p, side in zip(self.planes, self.sides):
            side.wait_recv()
            self.grad[p, 0, self.middle] += self.from_left[p, self.middle]
            if not self.final:
                self.middles.append(
                    self.copies.start(self.grad.at[p, 0, self.middle], self.from_right.at[p], left)
                )

    def corner(self):
        left = self.place.at(0, -1)
        self.corners = {}
        for p in self.planes:
            self.copies.sent(self.ups[p, 0])
            self.copies.sent(self.downs[p, 0])
            self.ups[p, 0].wait_recv()
            self.grad[p, 0, self.top] += self.from_up[p, 0]
            self.downs[p, 0].wait_recv()
            self.grad[p, 0, self.below] += self.from_down[p, 0]
            for k, lines in enumerate((self.top, self.below)):
                self.corners[p, k] = self.copies.start(
                    self.grad.at[p, 0, lines], self.from_corner.at[p, k], left
                )

    def update(self):
        grad, extended, last = self.grad, self.extended, self.last
        top, middle, below = self.top, self.middle, self.below
        for p in self.planes:
            extended[p % 2][p // 2, 0] -= STEP_OBJECT * grad[p, 0]
        for j in range(1, last):
            for p in self.planes:
                self.ups[p, j].wait_recv()
                self.downs[p, j].wait_recv()
                extended[p % 2][p // 2, j, middle] -= STEP_OBJECT * grad[p, j, middle]
                extended[p % 2][p // 2, j, top] -= STEP_OBJECT * (grad[p, j, top] + self.from_up[p, j])
                extended[p % 2][p // 2, j, below] -= STEP_OBJECT * (grad[p, j, below] + self.from_down[p, j])
        for p, copy in zip(self.planes, self.middles):
            copy.wait_recv()
            extended[p % 2][p // 2, last, middle] -= STEP_OBJECT * self.from_right[p]
            for k, lines in enumerate((top, below)):
                self.corners[p, k].wait_recv()
                extended[p % 2][p // 2, last, lines] -= STEP_OBJECT * self.from_corner[p, k]

    def keep(self, new_field):
        for j in range(self.last):
            for p in self.planes:
                new_field[p, :, self.block[j]] = (
                    self.extended[p % 2][p // 2, j, self.own] - STEP_OBJECT * self.grad[p, j, self.own]
                )

    def complete(self, new_field):
        for j in list(range(1, self.last)) + [0]:
            for p in self.planes:
                self.ups[p, j].wait_recv()
                new_field[p, self.top, self.block[j]] -= STEP_OBJECT * self.from_up[p, j]


SLICE_PLANES = ((0, 2), (1, 3))


def program_kernel(
    tiles,
    cols,
    rows,
    columns,
    counts,
    field,
    probe_hbm,
    measured_hbm,
    table_hbm,
    new_field,
    new_probe,
    object_first,
    object_second,
    grad,
    beam,
    grad_beam,
    measured,
    table,
    windows,
    spread,
    patches,
    from_left,
    from_up,
    from_right,
    from_down,
    from_corner,
    *rest,
):
    sums, (local_sem, send, recv) = rest[:-3], rest[-3:]
    sums = [sums[: len(sums) // 2], sums[len(sums) // 2 :]]
    extended = (object_first, object_second)
    planes, count, tall, size = grad.shape
    last = count - 1
    height = tall - size
    slots = measured.shape[0]
    step_probe = 1.0 / (slots * tiles * cols)
    top, below, own = pl.ds(0, size), pl.ds(height, size), pl.ds(0, height)
    block = [pl.ds(j * size, size) for j in range(last)]
    place = Place(tiles, cols)
    copies = Copies(send, recv)
    up, left = place.at(-1, 0), place.at(0, -1)

    loads = [
        (field.at[p, :, block[j]], extended[p % 2].at[p // 2, j, own])
        for p in range(planes)
        for j in range(last)
    ]
    loads += [(probe_hbm, beam), (table_hbm, table), (measured_hbm, measured)]
    loads = [
        pltpu.make_async_copy(source, target, local_sem.at[k])
        for k, (source, target) in enumerate(loads)
    ]
    for load in loads:
        load.start()
    greet(met(place))

    halos, sides, corners = {}, {}, {}

    def send_halo(p, j):
        halos[p, j] = copies.start(
            field.at[p, top, block[j]], extended[p % 2].at[p // 2, j, below], up
        )

    def pass_corners(which):
        for p in SLICE_PLANES[which]:
            halos[p, 0].wait_recv()
            corners[p] = copies.start(
                extended[p % 2].at[p // 2, 0, below], extended[p % 2].at[p // 2, last, below], left
            )

    def take_halo(which):
        for p in SLICE_PLANES[which]:
            for copy in [halos[p, j] for j in range(1, last)] + [sides[p], corners[p]]:
                copy.wait_recv()

    for which in SLICE_PLANES:
        for p in which:
            send_halo(p, 0)
        for p in which:
            sides[p] = copies.start(
                field.at[p, :, block[0]], extended[p % 2].at[p // 2, last, own], left
            )
        for j in range(1, last):
            for p in which:
                send_halo(p, j)
    pass_corners(0)
    for load in loads:
        load.wait()
    take_halo(0)

    refs = (rows, columns, counts, measured, extended, beam, table, grad, grad_beam)
    work = Positions(refs + (windows, spread, patches), size, slots)
    waiting = None
    for sweep in range(ITERS):
        final = sweep == ITERS - 1
        landed = (from_left.at[sweep], from_up.at[sweep], from_right, from_down, from_corner)
        zeroth, first = [
            Overlap(place, copies, which, grad, extended, landed, final) for which in SLICE_PLANES
        ]
        for step in range(work.groups):
            work.propagate(step)
            if step == 0 and sweep == 0:
                pass_corners(1)
        if sweep == 0:
            take_halo(1)
        else:
            waiting.update()
        copies.finish()
        grad_beam[...] = jnp.zeros_like(grad_beam)
        lax.fori_loop(0, work.groups, lambda step, carry: (work.diffract(step), carry)[1], 0)
        reduce = ProbeSum(place, copies, grad_beam, *sums[sweep])
        reduce.scatter_pair()
        for step in range(work.groups):
            work.place_patches(step, SLICE_PLANES[0])
            if step == 0:
                reduce.scatter_plane()
        zeroth.start()
        for step in range(work.groups):
            work.place_patches(step, SLICE_PLANES[1])
        first.start()
        zeroth.start_inner()
        first.start_inner()
        reduce.sum_line()
        zeroth.first()
        reduce.gather_plane()
        first.first()
        zeroth.inner()
        if final:
            first.inner()
            zeroth.keep(new_field)
            first.keep(new_field)
            zeroth.complete(new_field)
            reduce.gather_pair()
            first.complete(new_field)
            new_probe[...] = beam[...] - step_probe * reduce.result()
            copies.finish()
        else:
            zeroth.corner()
            first.inner()
            reduce.gather_pair()
            first.corner()
            zeroth.update()
            beam[...] -= step_probe * reduce.result()
            waiting = first


def local(table, tiles, cols, object_field, probe, row_offsets, col_offsets, counts, measured):
    size = probe.shape[-1]
    height, width = object_field.shape[2:]
    slots = row_offsets.shape[-1]
    field = object_field.reshape(4, height, width)
    flat = (probe.shape[0] * probe.shape[1] * size, size)
    planes, last, tall = 4, width // size, height + size
    needed = planes * (2 * last + 2) + ITERS * ProbeSum.copies_needed(tiles, cols)
    needed += planes * (3 + 2 * last + 1 + 2) + planes * (3 + last)
    work = ITERS * slots * probe.shape[1] * 8 * 3 * 2 * 256 * 256 * 128
    smem = pl.BlockSpec(memory_space=pltpu.SMEM)
    hbm = pl.BlockSpec(memory_space=pl.ANY)
    vmem = pl.BlockSpec(memory_space=pltpu.VMEM)
    new_field, new_probe = pl.pallas_call(
        functools.partial(program_kernel, tiles, cols),
        out_shape=[jax.ShapeDtypeStruct(field.shape, f32), jax.ShapeDtypeStruct(flat, f32)],
        in_specs=[smem] * 3 + [hbm] * 4,
        out_specs=[vmem] * 2,
        scratch_shapes=[
            pltpu.VMEM((planes // 2, last + 1, tall, size), f32),
            pltpu.VMEM((planes // 2, last + 1, tall, size), f32),
            pltpu.VMEM((planes, last + 1, tall, size), f32),
            pltpu.VMEM(flat, f32),
            pltpu.VMEM(flat, f32),
            pltpu.VMEM((slots, size, size), f32),
            pltpu.VMEM(table.shape, bf16),
            pltpu.VMEM((slots, 2, size, size), f32),
            pltpu.VMEM((slots, probe.shape[1], 2, size, size), f32),
            pltpu.VMEM((slots, planes, size, size), f32),
            pltpu.VMEM((ITERS, planes, tall, size), f32),
            pltpu.VMEM((ITERS, planes, last, size, size), f32),
            pltpu.VMEM((planes, height - size, size), f32),
            pltpu.VMEM((planes, last, size, size), f32),
            pltpu.VMEM((planes, 2, size, size), f32),
            *ProbeSum.scratch(*flat, tiles, cols),
            *ProbeSum.scratch(*flat, tiles, cols),
            pltpu.SemaphoreType.DMA((planes * last + 3,)),
            pltpu.SemaphoreType.DMA((needed,)),
            pltpu.SemaphoreType.DMA((needed,)),
        ],
        compiler_params=pltpu.CompilerParams(
            collective_id=0, has_side_effects=True, vmem_limit_bytes=VMEM_LIMIT
        ),
        cost_estimate=pl.CostEstimate(flops=work, bytes_accessed=5 * 2**20, transcendentals=0),
        name="ptychography",
    )(
        row_offsets.reshape(slots),
        col_offsets.reshape(slots),
        counts.reshape(1),
        field,
        probe.reshape(flat),
        measured.reshape(slots, size, size),
        table,
    )
    return new_field.reshape(object_field.shape), new_probe.reshape(probe.shape)


def solution(mesh):
    table = jnp.asarray(transform_tables(128))
    tiles, cols = mesh.shape["tiles"], mesh.shape["cols"]
    in_specs = (
        P(None, None, "tiles", "cols"),
        P(),
        P("tiles", "cols", None),
        P("tiles", "cols", None),
        P("tiles", "cols"),
        P("tiles", "cols", None, None, None),
    )
    out_specs = (P(None, None, "tiles", "cols"), P())
    body = functools.partial(local, table, tiles, cols)
    return jax.shard_map(body, mesh=mesh, in_specs=in_specs, out_specs=out_specs, check_vma=False)
```

profile of v0, /device:TPU:1, one launch (start us, length us, event | category | flops | bytes accessed | tf_op | source)
XLA Modules:
  0.0 109.5 jit_solution(17560121109704945323)
XLA Ops:
  1.3 105.1 %ptychography.1 = (f32[4,256,256]{2,1,0:T(8,128)}, f32[1024,128]{1,0:T(8,128)}) custom-call(s32[8]{0:T(128)} %bitcast.14, s32[8]{0:T(128)} %bitcast.15, s32[1]{0:T(128)} %bitcast.8.counts, f32[4,256,256]{2,1,0:T(8,128)} %bitcast.11, f32[1024,128]{1,0:T(8,128)} %bitcast.12, f32[8,128,128]{2,1,0:T(8,128)} %bitcast.13, bf16[8,256,256]{2,1,0:T(8,128)(2,1)} %constant.2.clone.table_hbm), custom_call_target="tpu_custom_call" | custom-call | flops 25769803776 | bytes 5242880 | tf_op jit(solution)/shard_map/ptychography/pallas_call | solution.py:630
  106.4 0.0 copy-start
  106.4 2.3 %copy.12 = f32[2,2,256,256]{3,2,1,0:T(8,128)} copy(f32[2,2,256,256]{3,2,1,0:T(8,128)} %bitcast.9) | data formatting | bytes 2097152
  108.8 0.0 copy-done
  108.8 0.8 copy.13
Async XLA Ops:
  106.4 2.4 %copy-start = (f32[1024,128]{1,0:T(8,128)S(1)}, f32[1024,128]{1,0:T(8,128)}, u32[]{:S(2)}) copy-start(f32[1024,128]{1,0:T(8,128)} %get-tuple-element.5) | copy-start | bytes 1572868
where the time goes:
time: 110 us
  Pallas kernels  105 us (95%)
  local copies, waits for them, and re-layouts  3.14 us (3%)
  between operations  1.29 us (1%)
    pallas_call x1, Pallas kernels, local(): pl.pallas_call(functools.partial(program_kernel, tiles, cols), out_shape=...  105 us
    unnamed x4, local copies, waits for them, and re-layouts  3.14 us

commit v1 on v0

--- a/solution.py
+++ b/solution.py
@@ -170,7 +170,7 @@
     def place_patches(self, step, planes):
         spots = self.spots(step)
         patches = [[self.patches[s[0], p] for p in planes] for s in spots]
-        self.put(spots, patches, planes, step == 0)
+        self.put(spots, patches, planes, isinstance(step, int) and step == 0)
 
     def put(self, spots, patches, planes, fresh):
         n = self.n
@@ -567,13 +567,14 @@
         zeroth, first = [
             Overlap(place, copies, which, grad, extended, landed, final) for which in SLICE_PLANES
         ]
-        for step in range(work.groups):
-            work.propagate(step)
-            if step == 0 and sweep == 0:
-                pass_corners(1)
         if sweep == 0:
+            for step in range(work.groups):
+                work.propagate(step)
+                if step == 0:
+                    pass_corners(1)
             take_halo(1)
         else:
+            lax.fori_loop(0, work.groups, lambda k, carry: (work.propagate(k), carry)[1], 0)
             waiting.update()
         copies.finish()
         grad_beam[...] = jnp.zeros_like(grad_beam)
@@ -585,8 +586,11 @@
             if step == 0:
                 reduce.scatter_plane()
         zeroth.start()
-        for step in range(work.groups):
-            work.place_patches(step, SLICE_PLANES[1])
+        for p in SLICE_PLANES[1]:
+            grad[p] = jnp.zeros(grad.shape[1:], f32)
+        lax.fori_loop(
+            0, work.groups, lambda k, carry: (work.place_patches(k, SLICE_PLANES[1]), carry)[1], 0
+        )
         first.start()
         zeroth.start_inner()
         first.start_inner()

time: 110 us -> 110 us (level)
  no operation moved by 1% of the time
where the time goes in v1:
time: 110 us
  Pallas kernels  105 us (95%)
  local copies, waits for them, and re-layouts  3.14 us (3%)
  between operations  1.29 us (1%)
    pallas_call x1, Pallas kernels, local(): pl.pallas_call(functools.partial(program_kernel, tiles, cols), out_shape=...  105 us
    unnamed x4, local copies, waits for them, and re-layouts  3.14 us

profile of v1, /device:TPU:1, one launch (start us, length us, event | category | flops | bytes accessed | tf_op | source)
XLA Modules:
  0.0 109.7 jit_solution(16377099779456366719)
XLA Ops:
  1.3 105.3 %ptychography.1 = (f32[4,256,256]{2,1,0:T(8,128)}, f32[1024,128]{1,0:T(8,128)}) custom-call(s32[8]{0:T(128)} %bitcast.14, s32[8]{0:T(128)} %bitcast.15, s32[1]{0:T(128)} %bitcast.8.counts, f32[4,256,256]{2,1,0:T(8,128)} %bitcast.11, f32[1024,128]{1,0:T(8,128)} %bitcast.12, f32[8,128,128]{2,1,0:T(8,128)} %bitcast.13, bf16[8,256,256]{2,1,0:T(8,128)(2,1)} %constant.2.clone.table_hbm), custom_call_target="tpu_custom_call" | custom-call | flops 25769803776 | bytes 5242880 | tf_op jit(solution)/shard_map/ptychography/pallas_call | solution.py:634
  106.5 0.0 copy-start
  106.5 2.3 %copy.12 = f32[2,2,256,256]{3,2,1,0:T(8,128)} copy(f32[2,2,256,256]{3,2,1,0:T(8,128)} %bitcast.9) | data formatting | bytes 2097152
  108.9 0.0 copy-done
  108.9 0.8 copy.13
Async XLA Ops:
  106.5 2.4 %copy-start = (f32[1024,128]{1,0:T(8,128)S(1)}, f32[1024,128]{1,0:T(8,128)}, u32[]{:S(2)}) copy-start(f32[1024,128]{1,0:T(8,128)} %get-tuple-element.5) | copy-start | bytes 1572868
